TPU v7x, 32 devices: a whole 2x2x4 slice. The times are simulated.
32 devices in a mesh: groups: 2 (over x), tile: 16 (over z, y, core).
Axes of the slice: x: 2, y: 2, z: 4, core: 2. Of those that a mesh axis runs over, the one named last changes fastest.
Arguments:
- model_field: float32 [16, 524288], P(None, ('groups', 'tile')), parts along dimension 1, may hold values from -6 to 6
- direction: float32 [16, 524288], P(None, ('groups', 'tile')), parts along dimension 1, may hold values from -100 to 100
- old_grad: float32 [16, 524288], P(None, ('groups', 'tile')), parts along dimension 1, may hold values from -100 to 100
- residual: float32 [16, 65536], P(None, ('groups', 'tile')), parts along dimension 1, may hold values from -6 to 6
- block_pairs: int32 [256, 8], P(('groups', 'tile')), parts along dimension 0, may hold values from 0 to 159, as said below
- depth_band: int32 [524288], P(('groups', 'tile')), parts along dimension 0, may hold values from 0 to 15
- station_offsets: float32 [2, 65536], P(None, ('groups', 'tile')), parts along dimension 1, may hold values from -1.25 to 2.25, as said below
Outputs:
- new_model: float32 [16, 524288], P(None, ('groups', 'tile')), parts along dimension 1
- new_residual: float32 [16, 65536], P(None, ('groups', 'tile')), parts along dimension 1
- new_direction: float32 [16, 524288], P(None, ('groups', 'tile')), parts along dimension 1
There are 2 independent parts, one for each index of `groups`. A program takes and returns all parts, laid end to end along the dimension named above; each array names one. Nothing has to cross between parts.
Inputs may be any that keep to these rules, and one draw needn't show every extreme that they name: `block_pairs`: each row lists 8 different codes. `station_offsets`: row 1 (along) lies between 0 and 1.
All inputs are finite; a program needn't handle non-finite values.
Results may differ from a plain program's by a relative error of at most 0.0003.
Values sent between devices are 32-bit elements; how exact they have to be, the bound alone decides.
No kernel may reach another device: no remote copies, remote signals or barrier semaphores. Data moves between devices by JAX's collectives and lax.ppermute only.
A program may use at most 128 MiB of HBM per device.

v0:
```python
import math

import jax
import jax.numpy as jnp
from jax import lax
from jax.sharding import PartitionSpec as P

CBLOCK = 512
SBLOCK = 256
REACH = 2
BANDS = 16
COL_SIDE = 32


HIGHEST = lax.Precision.HIGHEST
DEPTH_RANGE = 2.0
DEPTH_SHIFT = 0.25
DAMPING = 1.0
GUARD = 1e-06


def passed_along(array, axis, by):
    length = lax.axis_size(axis)
    pairs = [(i, i + by) for i in range(length) if 0 <= i + by < length]
    return lax.ppermute(array, axis, pairs)


def point_kernel(station_across, station_along, cell_across, cell_along, cell_depth):
    across_gap = station_across[..., :, None] - cell_across[..., None, :]
    along_gap = station_along[..., :, None] - cell_along[..., None, :]
    depth_column = cell_depth[..., None, :]
    inverse = lax.rsqrt(
        across_gap * across_gap + along_gap * along_gap + depth_column * depth_column
    )
    return depth_column * inverse * inverse * inverse


def shards(model_field, direction, old_grad, residual, block_pairs, depth_band, station_offsets):
    tile_id = lax.axis_index("tile")
    tile_float = tile_id.astype(jnp.float32)
    epochs, cells = model_field.shape
    stations = residual.shape[1]
    station_blocks = block_pairs.shape[0]
    cell_blocks = cells // CBLOCK
    kernel_scale = 2.0 / math.sqrt(cells)
    cell_index = jnp.arange(cells, dtype=jnp.int32)
    column = cell_index % (COL_SIDE * COL_SIDE)
    local_across = ((column % COL_SIDE).astype(jnp.float32) + 0.5) / COL_SIDE
    local_along = ((column // COL_SIDE).astype(jnp.float32) + 0.5) / COL_SIDE
    cell_depth = (depth_band.astype(jnp.float32) + 0.5) * (DEPTH_RANGE / BANDS)
    weight = (cell_depth + DEPTH_SHIFT) ** 1.5
    across_blocks = local_across.reshape(cell_blocks, CBLOCK)
    along_blocks = local_along.reshape(cell_blocks, CBLOCK)
    across_flat = station_offsets[0] + tile_float
    station_across = across_flat.reshape(station_blocks, SBLOCK)
    station_along = station_offsets[1].reshape(station_blocks, SBLOCK)
    weighted = weight[None, :] * direction
    span_blocks = (2 * REACH + 1) * cell_blocks
    nearby = []
    for offset in range(-REACH, REACH + 1):
        if offset == 0:
            nearby.append((weighted, cell_depth))
        else:
            nearby.append(passed_along((weighted, cell_depth), "tile", -offset))
    near_values = jnp.stack([member[0] for member in nearby], axis=1).reshape(
        epochs, span_blocks, CBLOCK
    )
    near_depth = jnp.stack([member[1] for member in nearby], axis=0).reshape(span_blocks, CBLOCK)

    def block_kernel(code_list, across_row, along_row):
        within = code_list % cell_blocks
        moved = (code_list // cell_blocks - REACH).astype(jnp.float32) + tile_float
        cell_across = jnp.take(across_blocks, within, axis=0) + moved[:, None]
        cell_along = jnp.take(along_blocks, within, axis=0)
        block_depth = jnp.take(near_depth, code_list, axis=0)
        return (
            point_kernel(
                across_row[None, :], along_row[None, :], cell_across, cell_along, block_depth
            )
            * kernel_scale
        )

    def forward_block(inputs):
        code_list, across_row, along_row = inputs
        matrix = block_kernel(code_list, across_row, along_row)
        gathered = jnp.take(near_values, code_list, axis=1)
        return jnp.einsum(
            "epc,psc->es", gathered, matrix, precision=HIGHEST, preferred_element_type=jnp.float32
        )

    image_blocks = lax.map(forward_block, (block_pairs, station_across, station_along))
    image_data = jnp.transpose(image_blocks, (1, 0, 2)).reshape(epochs, stations)
    gamma_old, direction_norm, image_norm = lax.psum(
        (
            jnp.sum(old_grad * old_grad),
            jnp.sum(direction * direction),
            jnp.sum(image_data * image_data),
        ),
        "tile",
    )
    step_length = gamma_old / (image_norm + DAMPING * direction_norm + GUARD)
    new_model = model_field + step_length * direction
    new_residual = residual - step_length * image_data
    row_count = new_residual.shape[0]
    station_pieces = jnp.transpose(
        new_residual.reshape(row_count, station_blocks, SBLOCK), (1, 0, 2)
    )

    def adjoint_step(accumulated, inputs):
        code_list, station_values, across_row, along_row = inputs
        matrix = block_kernel(code_list, across_row, along_row)
        contribution = jnp.einsum(
            "es,psc->epc",
            station_values,
            matrix,
            precision=HIGHEST,
            preferred_element_type=jnp.float32,
        )
        return (accumulated.at[:, code_list, :].add(contribution), None)

    accumulated, unused = lax.scan(
        adjoint_step,
        jnp.zeros((row_count, span_blocks, CBLOCK), jnp.float32),
        (block_pairs, station_pieces, station_across, station_along),
    )
    slab_stack = accumulated.reshape(row_count, 2 * REACH + 1, cells)

    def slab_at(offset):
        return slab_stack[:, offset + REACH, :]

    summed = slab_at(0)
    for offset in range(-REACH, REACH + 1):
        if offset != 0:
            summed = summed + passed_along(slab_at(offset), "tile", offset)
    gradient = weight[None, :] * summed - DAMPING * new_model
    gamma_new = lax.psum(jnp.sum(gradient * gradient), "tile")
    new_direction = gradient + gamma_new / (gamma_old + GUARD) * direction
    return (new_model, new_residual, new_direction)


def solution(mesh):
    return jax.shard_map(
        shards,
        mesh=mesh,
        in_specs=(
            P(None, ("groups", "tile")),
            P(None, ("groups", "tile")),
            P(None, ("groups", "tile")),
            P(None, ("groups", "tile")),
            P(("groups", "tile"), None),
            P(("groups", "tile")),
            P(None, ("groups", "tile")),
        ),
        out_specs=(
            P(None, ("groups", "tile")),
            P(None, ("groups", "tile")),
            P(None, ("groups", "tile")),
        ),
        check_vma=False,
    )
```

profile of v0, /device:TPU:0, one launch (start us, length us, event | category | flops | bytes accessed | tf_op | source)
XLA Modules:
  0.0 431.0 jit_solution(15693981275816197951)
XLA Ops:
  3.6 4.9 %collective-permute-start = (f32[16,16384]{1,0:T(8,128)S(1)}, f32[16,16384]{1,0:T(8,128)S(1)}, u32[]{:S(2)}, u32[]{:S(2)}) collective-permute-start(f32[16,16384]{1,0:T(8,128)S(1)} %get-tuple-element.382), channel_id=1, source_target_pairs={{0,2},{1,3},{2,4},{3,5},{4,6},{5,7},{6,8},{7,9},{8,10},{9,11},{10,... | collective-permute-start | bytes 3145736 | tf_op jit(solution)/shard_map/ppermute | solution.py:25
  8.6 3.4 collective-permute-start.4
  18.8 16.3 %collective-permute-done.4 = f32[16384]{0:T(1024)S(1)} collective-permute-done((f32[16384]{0:T(1024)S(1)}, f32[16384]{0:T(1024)S(1)}, u32[]{:S(2)}, u32[]{:S(2)}) %collective-permute-start.4) | collective-permute-done | bytes 65568 | tf_op jit(solution)/shard_map/ppermute | solution.py:25
  45.1 33.4 %collective-permute-done.3 = f32[16,16384]{1,0:T(8,128)} collective-permute-done((f32[16,16384]{1,0:T(8,128)S(1)}, f32[16,16384]{1,0:T(8,128)}, u32[]{:S(2)}, u32[]{:S(2)}) %collective-permute-start.3) | collective-permute-done | bytes 1048608 | tf_op jit(solution)/shard_map/ppermute | solution.py:25
  79.8 6.5 %copy.13 = f32[16,5,16384]{2,1,0:T(8,128)} copy(f32[16,5,16384]{2,0,1:T(8,128)S(1)} %bitcast_dynamic-update-slice_fusion) | data formatting | bytes 10485760 | tf_op jit(solution)/shard_map/stack | solution.py:65
  86.2 8.4 %reshape.213 = f32[16,160,512]{2,1,0:T(8,128)} reshape(f32[16,5,16384]{2,1,0:T(8,128)} %copy.13) | data formatting | bytes 10485760 | tf_op jit(solution)/shard_map/reshape | solution.py:65
  94.6 7.8 %copy.14 = f32[16,160,512]{2,0,1:T(8,128)} copy(f32[16,160,512]{2,1,0:T(8,128)} %reshape.213) | data formatting | bytes 10485760
  102.4 75.8 %while.26 = (s32[]{:T(128)}, f32[8,16,256]{2,1,0:T(8,128)S(1)}, s32[8,8]{1,0:T(8,128)S(1)}, f32[16,160,512]{2,0,1:T(8,128)}, f32[160,512]{1,0:T(8,128)S(1)}, /*i...) while((s32[]{:T(128)}, f32[8,16,256]{2,1,0:T(8,128)S(1)}, ...), condition=%wide.region_3.6_spmd.clone, body=%wide.region_2.5_spmd.clone.sunk | while | flops 212852080 | bytes 1232045 | solution.py:91
  107.6 4.4 %fusion.106 = f32[8,16,256]{2,1,0:T(8,128)S(1)} fusion(f32[8,16,256]{2,1,0:T(8,128)S(1)} %get-tuple-element.537, s32[]{:T(128)} %get-tuple-element.536, f32[8,512]{1,0:T(8,128)S(1)} %get-tuple-element.501, f32[8,512]{1,0:T(8,128)S(1)} %get-tuple-element.502, f32[256]{0:T(256)S(1)} %bitcast.161, f32[8,512]{1,0:T(8,128)S(1)} %get-tuple-element.504, ...), kind=kOutput, calls=%fused_computation.30.clone.1 | convolution fusion | flops 211877888 | bytes 346628 | tf_op jit(solution)/shard_map/while/body/eval_jaxpr/epc,psc->es/dot_general | solution.py:87
  117.0 4.4 %fusion.106 = f32[8,16,256]{2,1,0:T(8,128)S(1)} fusion(f32[8,16,256]{2,1,0:T(8,128)S(1)} %get-tuple-element.537, s32[]{:T(128)} %get-tuple-element.536, f32[8,512]{1,0:T(8,128)S(1)} %get-tuple-element.501, f32[8,512]{1,0:T(8,128)S(1)} %get-tuple-element.502, f32[256]{0:T(256)S(1)} %bitcast.161, f32[8,512]{1,0:T(8,128)S(1)} %get-tuple-element.504, ...), kind=kOutput, calls=%fused_computation.30.clone.1 | convolution fusion | flops 211877888 | bytes 346628 | tf_op jit(solution)/shard_map/while/body/eval_jaxpr/epc,psc->es/dot_general | solution.py:87
  126.5 4.4 %fusion.106 = f32[8,16,256]{2,1,0:T(8,128)S(1)} fusion(f32[8,16,256]{2,1,0:T(8,128)S(1)} %get-tuple-element.537, s32[]{:T(128)} %get-tuple-element.536, f32[8,512]{1,0:T(8,128)S(1)} %get-tuple-element.501, f32[8,512]{1,0:T(8,128)S(1)} %get-tuple-element.502, f32[256]{0:T(256)S(1)} %bitcast.161, f32[8,512]{1,0:T(8,128)S(1)} %get-tuple-element.504, ...), kind=kOutput, calls=%fused_computation.30.clone.1 | convolution fusion | flops 211877888 | bytes 346628 | tf_op jit(solution)/shard_map/while/body/eval_jaxpr/epc,psc->es/dot_general | solution.py:87
  136.0 4.4 %fusion.106 = f32[8,16,256]{2,1,0:T(8,128)S(1)} fusion(f32[8,16,256]{2,1,0:T(8,128)S(1)} %get-tuple-element.537, s32[]{:T(128)} %get-tuple-element.536, f32[8,512]{1,0:T(8,128)S(1)} %get-tuple-element.501, f32[8,512]{1,0:T(8,128)S(1)} %get-tuple-element.502, f32[256]{0:T(256)S(1)} %bitcast.161, f32[8,512]{1,0:T(8,128)S(1)} %get-tuple-element.504, ...), kind=kOutput, calls=%fused_computation.30.clone.1 | convolution fusion | flops 211877888 | bytes 346628 | tf_op jit(solution)/shard_map/while/body/eval_jaxpr/epc,psc->es/dot_general | solution.py:87
  145.5 4.4 %fusion.106 = f32[8,16,256]{2,1,0:T(8,128)S(1)} fusion(f32[8,16,256]{2,1,0:T(8,128)S(1)} %get-tuple-element.537, s32[]{:T(128)} %get-tuple-element.536, f32[8,512]{1,0:T(8,128)S(1)} %get-tuple-element.501, f32[8,512]{1,0:T(8,128)S(1)} %get-tuple-element.502, f32[256]{0:T(256)S(1)} %bitcast.161, f32[8,512]{1,0:T(8,128)S(1)} %get-tuple-element.504, ...), kind=kOutput, calls=%fused_computation.30.clone.1 | convolution fusion | flops 211877888 | bytes 346628 | tf_op jit(solution)/shard_map/while/body/eval_jaxpr/epc,psc->es/dot_general | solution.py:87
  154.9 4.4 %fusion.106 = f32[8,16,256]{2,1,0:T(8,128)S(1)} fusion(f32[8,16,256]{2,1,0:T(8,128)S(1)} %get-tuple-element.537, s32[]{:T(128)} %get-tuple-element.536, f32[8,512]{1,0:T(8,128)S(1)} %get-tuple-element.501, f32[8,512]{1,0:T(8,128)S(1)} %get-tuple-element.502, f32[256]{0:T(256)S(1)} %bitcast.161, f32[8,512]{1,0:T(8,128)S(1)} %get-tuple-element.504, ...), kind=kOutput, calls=%fused_computation.30.clone.1 | convolution fusion | flops 211877888 | bytes 346628 | tf_op jit(solution)/shard_map/while/body/eval_jaxpr/epc,psc->es/dot_general | solution.py:87
  164.4 4.4 %fusion.106 = f32[8,16,256]{2,1,0:T(8,128)S(1)} fusion(f32[8,16,256]{2,1,0:T(8,128)S(1)} %get-tuple-element.537, s32[]{:T(128)} %get-tuple-element.536, f32[8,512]{1,0:T(8,128)S(1)} %get-tuple-element.501, f32[8,512]{1,0:T(8,128)S(1)} %get-tuple-element.502, f32[256]{0:T(256)S(1)} %bitcast.161, f32[8,512]{1,0:T(8,128)S(1)} %get-tuple-element.504, ...), kind=kOutput, calls=%fused_computation.30.clone.1 | convolution fusion | flops 211877888 | bytes 346628 | tf_op jit(solution)/shard_map/while/body/eval_jaxpr/epc,psc->es/dot_general | solution.py:87
  173.9 4.4 %fusion.106 = f32[8,16,256]{2,1,0:T(8,128)S(1)} fusion(f32[8,16,256]{2,1,0:T(8,128)S(1)} %get-tuple-element.537, s32[]{:T(128)} %get-tuple-element.536, f32[8,512]{1,0:T(8,128)S(1)} %get-tuple-element.501, f32[8,512]{1,0:T(8,128)S(1)} %get-tuple-element.502, f32[256]{0:T(256)S(1)} %bitcast.161, f32[8,512]{1,0:T(8,128)S(1)} %get-tuple-element.504, ...), kind=kOutput, calls=%fused_computation.30.clone.1 | convolution fusion | flops 211877888 | bytes 346628 | tf_op jit(solution)/shard_map/while/body/eval_jaxpr/epc,psc->es/dot_general | solution.py:87
  180.2 39.2 %all-reduce = (f32[]{:T(128)}, f32[]{:T(128)}) all-reduce(f32[]{:T(128)} %multiply_reduce_fusion.2, f32[]{:T(128)S(6)} %add.299), channel_id=1, replica_groups=mesh['groups'=2,'tile'=16] {'tile'}, use_global_device_ids=true, to_apply=%region_1.2 | all-reduce | flops 2 | bytes 16 | tf_op jit(solution)/shard_map/psum | solution.py:93
  223.8 63.3 %while.27 = (s32[]{:T(128)}, f32[16,160,512]{2,0,1:T(8,128)}, s32[8,8]{1,0:T(8,128)S(1)}, f32[8,16,256]{2,1,0:T(8,128)S(1)}, f32[160,512]{1,0:T(8,128)S(1)}, /*i...) while((s32[]{:T(128)}, f32[16,160,512]{2,0,1:T(8,128)}, ...), condition=%wide.region_10.13_spmd.clone, body=%wide.region_8.12_spmd.clone.sunk | while | flops 212851056 | bytes 1489549 | solution.py:121
  225.8 3.6 fusion.112
  233.7 3.6 fusion.112
  241.6 3.6 fusion.112
  249.5 3.6 fusion.112
  257.5 3.6 fusion.112
  265.4 3.6 fusion.112
  273.3 3.6 fusion.112
  281.2 3.6 fusion.112
  287.1 7.9 %copy.17 = f32[16,160,512]{2,1,0:T(8,128)} copy(f32[16,160,512]{2,0,1:T(8,128)} %get-tuple-element.264) | data formatting | bytes 10485760 | tf_op jit(solution)/shard_map/while | solution.py:121
  295.0 8.0 %reshape.216 = f32[16,5,16384]{2,1,0:T(8,128)} reshape(f32[16,160,512]{2,1,0:T(8,128)} %copy.17) | data formatting | bytes 10485760 | tf_op jit(solution)/shard_map/reshape | solution.py:126
  303.1 19.8 %fusion.88 = (f32[16,1,16384]{2,1,0:T(1,128)S(1)}, f32[16,1,16384]{2,1,0:T(1,128)S(1)}, f32[16,1,16384]{2,1,0:T(1,128)S(1)}, f32[16,1,16384]{2,1,0:T(1,128)}, f32[16,1,16384]{2,1,0:T(1,128)}) fusion(f32[16,5,16384]{2,1,0:T(8,128)} %reshape.216), kind=kLoop, calls=%fused_computation.169 | loop fusion | bytes 10485760 | tf_op jit(solution)/shard_map/slice | solution.py:129
  339.6 50.2 %collective-permute-done.11 = f32[16,16384]{1,0:T(8,128)} collective-permute-done((f32[16,16384]{1,0:T(8,128)}, f32[16,16384]{1,0:T(8,128)}, u32[]{:S(2)}, u32[]{:S(2)}) %collective-permute-start.11) | collective-permute-done | bytes 1048608 | tf_op jit(solution)/shard_map/ppermute | solution.py:25
  390.7 4.9 %multiply_reduce_fusion = (f32[]{:T(128)}, f32[16,16384]{1,0:T(8,128)S(1)}, f32[16,16384]{1,0:T(8,128)}) fusion(f32[16,16384]{1,0:T(8,128)} %collective-permute-done.11, f32[16,16384]{1,0:T(8,128)} %collective-permute-done.10, f32[16,16384]{1,0:T(8,128)} %collective-permute-done.9, f32[16,16384]{1,0:T(8,128)} %copy-done.1, ...), kind=kLoop, calls=%fused_computation.155 | loop fusion | flops 2621439 | bytes 9502728 | tf_op jit(solution)/shard_map/reduce_sum | solution.py:136
  395.7 33.6 %psum.31 = f32[]{:T(128)} all-reduce(f32[]{:T(128)} %get-tuple-element.359), channel_id=1, replica_groups=mesh['groups'=2,'tile'=16] {'tile'}, use_global_device_ids=true, to_apply=%region_12.15 | all-reduce | flops 1 | bytes 8 | tf_op jit(solution)/shard_map/psum | solution.py:136
  (286 shorter events, 117.0 us)
Async XLA Ops:
  3.6 37.1 %collective-permute-start = (f32[16,16384]{1,0:T(8,128)S(1)}, f32[16,16384]{1,0:T(8,128)S(1)}, u32[]{:S(2)}, u32[]{:S(2)}) collective-permute-start(f32[16,16384]{1,0:T(8,128)S(1)} %get-tuple-element.382), channel_id=1, source_target_pairs={{0,2},{1,3},{2,4},{3,5},{4,6},{5,7},{6,8},{7,9},{8,10},{9,11},{10,... | collective-permute-start | bytes 3145736 | tf_op jit(solution)/shard_map/ppermute | solution.py:25
  8.6 26.5 %collective-permute-start.4 = (f32[16384]{0:T(1024)S(1)}, f32[16384]{0:T(1024)S(1)}, u32[]{:S(2)}, u32[]{:S(2)}) collective-permute-start(f32[16384]{0:T(1024)S(1)} %get-tuple-element.383), channel_id=1, source_target_pairs={{0,2},{1,3},{2,4},{3,5},{4,6},{5,7},{6,8},{7,9},{8,10},{9,11},{10,... | collective-permute-start | bytes 196616 | tf_op jit(solution)/shard_map/ppermute | solution.py:25
  11.9 25.4 %collective-permute-start.5 = (f32[16384]{0:T(1024)S(1)}, f32[16384]{0:T(1024)S(1)}, u32[]{:S(2)}, u32[]{:S(2)}) collective-permute-start(f32[16384]{0:T(1024)S(1)} %get-tuple-element.383), channel_id=1, source_target_pairs={{0,1},{1,2},{2,3},{3,4},{4,5},{5,6},{6,7},{7,8},{8,9},{9,10},{10,1... | collective-permute-start | bytes 196616 | tf_op jit(solution)/shard_map/ppermute | solution.py:25
  13.2 25.4 %collective-permute-start.6 = (f32[16384]{0:T(1024)S(1)}, f32[16384]{0:T(1024)S(1)}, u32[]{:S(2)}, u32[]{:S(2)}) collective-permute-start(f32[16384]{0:T(1024)S(1)} %get-tuple-element.383), channel_id=1, source_target_pairs={{1,0},{2,1},{3,2},{4,3},{5,4},{6,5},{7,6},{8,7},{9,8},{10,9},{11,1... | collective-permute-start | bytes 196616 | tf_op jit(solution)/shard_map/ppermute | solution.py:25
  14.5 25.4 %collective-permute-start.7 = (f32[16384]{0:T(1024)S(1)}, f32[16384]{0:T(1024)S(1)}, u32[]{:S(2)}, u32[]{:S(2)}) collective-permute-start(f32[16384]{0:T(1024)S(1)} %get-tuple-element.383), channel_id=1, source_target_pairs={{2,0},{3,1},{4,2},{5,3},{6,4},{7,5},{8,6},{9,7},{10,8},{11,9},{12,... | collective-permute-start | bytes 196616 | tf_op jit(solution)/shard_map/ppermute | solution.py:25
  35.1 5.7 %collective-permute-start.1 = (f32[16,16384]{1,0:T(8,128)S(1)}, f32[16,16384]{1,0:T(8,128)}, u32[]{:S(2)}, u32[]{:S(2)}) collective-permute-start(f32[16,16384]{1,0:T(8,128)S(1)} %get-tuple-element.382), channel_id=1, source_target_pairs={{0,1},{1,2},{2,3},{3,4},{4,5},{5,6},{6,7},{7,8},{8,9},{9,10},{10,1... | collective-permute-start | bytes 3145736 | tf_op jit(solution)/shard_map/ppermute | solution.py:25
  37.4 6.4 %collective-permute-start.2 = (f32[16,16384]{1,0:T(8,128)S(1)}, f32[16,16384]{1,0:T(8,128)}, u32[]{:S(2)}, u32[]{:S(2)}) collective-permute-start(f32[16,16384]{1,0:T(8,128)S(1)} %get-tuple-element.382), channel_id=1, source_target_pairs={{1,0},{2,1},{3,2},{4,3},{5,4},{6,5},{7,6},{8,7},{9,8},{10,9},{11,1... | collective-permute-start | bytes 3145736 | tf_op jit(solution)/shard_map/ppermute | solution.py:25
  38.7 39.8 %collective-permute-start.3 = (f32[16,16384]{1,0:T(8,128)S(1)}, f32[16,16384]{1,0:T(8,128)}, u32[]{:S(2)}, u32[]{:S(2)}) collective-permute-start(f32[16,16384]{1,0:T(8,128)S(1)} %get-tuple-element.382), channel_id=1, source_target_pairs={{2,0},{3,1},{4,2},{5,3},{6,4},{7,5},{8,6},{9,7},{10,8},{11,9},{12,... | collective-permute-start | bytes 3145736 | tf_op jit(solution)/shard_map/ppermute | solution.py:25
  94.6 7.8 %copy-start.4 = (s32[8,8]{1,0:T(8,128)S(1)}, s32[8,8]{1,0:T(8,128)}, u32[]{:S(2)}) copy-start(s32[8,8]{1,0:T(8,128)} %param.19) | copy-start | bytes 772
  102.4 118.3 %copy-start.3 = (f32[16,2048]{1,0:T(8,128)S(1)}, f32[16,2048]{1,0:T(8,128)}, u32[]{:S(2)}) copy-start(f32[16,2048]{1,0:T(8,128)} %param.18) | copy-start | bytes 393220
  220.8 3.0 copy-start.2
  322.9 67.9 %copy-start = (f32[16,16384]{1,0:T(8,128)S(1)}, f32[16,16384]{1,0:T(8,128)}, u32[]{:S(2)}) copy-start(f32[16,16384]{1,0:T(8,128)} %param.16) | copy-start | bytes 3145732
  325.8 13.8 %collective-permute-start.10 = (f32[16,16384]{1,0:T(8,128)}, f32[16,16384]{1,0:T(8,128)}, u32[]{:S(2)}, u32[]{:S(2)}) collective-permute-start(f32[16,16384]{1,0:T(8,128)} %bitcast.115), channel_id=1, source_target_pairs={{0,1},{1,2},{2,3},{3,4},{4,5},{5,6},{6,7},{7,8},{8,9},{9,10},{10,1... | collective-permute-start | bytes 3145736 | tf_op jit(solution)/shard_map/ppermute | solution.py:25
  330.9 58.8 %collective-permute-start.11 = (f32[16,16384]{1,0:T(8,128)}, f32[16,16384]{1,0:T(8,128)}, u32[]{:S(2)}, u32[]{:S(2)}) collective-permute-start(f32[16,16384]{1,0:T(8,128)} %bitcast.118), channel_id=1, source_target_pairs={{0,2},{1,3},{2,4},{3,5},{4,6},{5,7},{6,8},{7,9},{8,10},{9,11},{10,... | collective-permute-start | bytes 3145736 | tf_op jit(solution)/shard_map/ppermute | solution.py:25
  334.8 55.0 %collective-permute-start.8 = (f32[16,16384]{1,0:T(8,128)}, f32[16,16384]{1,0:T(8,128)S(1)}, u32[]{:S(2)}, u32[]{:S(2)}) collective-permute-start(f32[16,16384]{1,0:T(8,128)} %bitcast.117), channel_id=1, source_target_pairs={{2,0},{3,1},{4,2},{5,3},{6,4},{7,5},{8,6},{9,7},{10,8},{11,9},{12,... | collective-permute-start | bytes 3145736 | tf_op jit(solution)/shard_map/ppermute | solution.py:25
  337.6 52.1 %collective-permute-start.9 = (f32[16,16384]{1,0:T(8,128)}, f32[16,16384]{1,0:T(8,128)}, u32[]{:S(2)}, u32[]{:S(2)}) collective-permute-start(f32[16,16384]{1,0:T(8,128)} %bitcast.116), channel_id=1, source_target_pairs={{1,0},{2,1},{3,2},{4,3},{5,4},{6,5},{7,6},{8,7},{9,8},{10,9},{11,1... | collective-permute-start | bytes 3145736 | tf_op jit(solution)/shard_map/ppermute | solution.py:25
  389.8 1.0 copy-start.1
where the time goes:
time: 433 us; the launch traced here: 431 us
  local copies, waits for them, and re-layouts  128 us (30%)
  waiting for transfers between devices  101 us (23%)
  blocking collectives  72.8 us (17%)
  matrix products  63.8 us (15%)
  other arithmetic  35.3 us (8%)
  starting transfers between devices  24.1 us (6%)
  between operations  4.77 us (1%)
    ppermute x12, waiting for transfers between devices, passed_along(): return lax.ppermute(array, axis, pairs)  101 us
    psum x1, blocking collectives, shards(): lax.psum((jnp.sum(old_grad * old_grad), jnp.sum(direction * direction), j...  39.2 us
    dot_general x8, matrix products, forward_block(): jnp.einsum('epc,psc->es', gathered, matrix, precision=HIGHEST, preferred_...  34.8 us
    psum x1, blocking collectives, shards(): gamma_new = lax.psum(jnp.sum(gradient * gradient), 'tile')  33.6 us
    dot_general x8, matrix products, adjoint_step(): jnp.einsum('es,psc->epc', station_values, matrix, precision=HIGHEST, pref...  29 us
    gather x8, local copies, waits for them, and re-layouts, forward_block(): gathered = jnp.take(near_values, code_list, axis=1)  24.4 us
    ppermute x12, starting transfers between devices, passed_along(): return lax.ppermute(array, axis, pairs)  24.1 us
    unnamed x19, local copies, waits for them, and re-layouts  20.4 us
  transfers between devices with their start and end apart: 12, of which 4 were waited for; matrix products, arithmetic and copies ran while one was open for 3% of the time, Pallas kernels for 0%

commit v1 on v0

v1 whole, which is shorter than its diff:
```python
import functools
import math

import jax
import jax.numpy as jnp
from jax import lax
from jax.experimental import pallas as pl
from jax.experimental.pallas import tpu as pltpu
from jax.sharding import PartitionSpec as P

CBLOCK = 512
SBLOCK = 256
REACH = 2
BANDS = 16
COL_SIDE = 32
DEPTH_RANGE = 2.0
DEPTH_SHIFT = 0.25
DAMPING = 1.0
GUARD = 1e-06

F32 = jnp.float32
BF16 = jnp.bfloat16
SLOTS = 2 * REACH + 1
LANES = 128

SMEM = pl.BlockSpec(memory_space=pltpu.SMEM)
VMEM = pl.BlockSpec(memory_space=pltpu.VMEM)


def params():
    return pltpu.CompilerParams(vmem_limit_bytes=48 * 2**20)


def split(values):
    high = values.astype(BF16)
    return high, (values - high.astype(F32)).astype(BF16)


def dot(left, right):
    return jnp.dot(left, right, preferred_element_type=F32)


def prepare_kernel(scale, band_ref, band_row_ref, direction_ref, old_ref, values_ref, cells_ref, turned_ref, sums_ref):
    blocks = values_ref.shape[0]
    epochs = direction_ref.shape[0]
    depth = (band_ref[...].astype(F32) + 0.5) * (DEPTH_RANGE / BANDS)
    turned_ref[...] = (depth * depth).T

    def block(w, sums):
        at = pl.ds(pl.multiple_of(w * CBLOCK, CBLOCK), CBLOCK)
        row = (band_row_ref[:, at].astype(F32) + 0.5) * (DEPTH_RANGE / BANDS)
        shifted = row + DEPTH_SHIFT
        factor = row * scale * (shifted * jnp.sqrt(shifted))
        cells_ref[pl.ds(0, 1), at] = row * row
        cells_ref[pl.ds(1, 1), at] = factor
        values = direction_ref[:, at]
        old = old_ref[:, at]
        high, low = split(values * factor)
        values_ref[w, pl.ds(0, epochs), :] = high
        values_ref[w, pl.ds(epochs, epochs), :] = low
        return sums[0] + old * old, sums[1] + values * values

    zero = jnp.zeros((epochs, CBLOCK), F32)
    old_sum, direction_sum = lax.fori_loop(0, blocks, block, (zero, zero), unroll=2)
    sums_ref[pl.ds(0, 1), :] = jnp.broadcast_to(jnp.sum(old_sum).reshape(1, 1), (1, LANES))
    sums_ref[pl.ds(1, 1), :] = jnp.broadcast_to(jnp.sum(direction_sum).reshape(1, 1), (1, LANES))


def prepare(scale, depth_band, direction, old_grad):
    epochs, cells = direction.shape
    blocks = cells // CBLOCK
    return pl.pallas_call(
        functools.partial(prepare_kernel, scale),
        out_shape=(
            jax.ShapeDtypeStruct((blocks, 2 * epochs, CBLOCK), BF16),
            jax.ShapeDtypeStruct((2, cells), F32),
            jax.ShapeDtypeStruct((cells // LANES, LANES), F32),
            jax.ShapeDtypeStruct((2, LANES), F32),
        ),
        in_specs=[VMEM] * 4,
        out_specs=(VMEM,) * 4,
        compiler_params=params(),
        cost_estimate=pl.CostEstimate(flops=8 * epochs * cells, bytes_accessed=12 * epochs * cells, transcendentals=0),
        name="prepare",
    )(depth_band.reshape(cells // LANES, LANES), depth_band.reshape(1, cells), direction, old_grad)


def list_pairs(slot, first_ref, codes_ref, list_ref, count, cell_blocks, station_blocks, pairs):
    first = first_ref[slot]
    for i in range(station_blocks * pairs):
        within = codes_ref[2, i].astype(jnp.int32) - first
        hit = jnp.logical_and(within >= 0, within < cell_blocks)
        list_ref[count] = (slot * station_blocks + i // pairs) * cell_blocks + within
        count = count + hit.astype(jnp.int32)
    return count


def pipelined(count, build, multiply, buffers):
    (high0, low0), (high1, low1) = buffers

    def step(j, unused):
        build(2 * j + 1, high1, low1)
        multiply(2 * j, high0, low0)
        build(2 * j + 2, high0, low0)
        multiply(2 * j + 1, high1, low1)
        return 0

    build(0, high0, low0)
    lax.fori_loop(0, (count + 1) // 2, step, 0)


def inverse_cube(squared):
    return lax.rsqrt(squared * squared * squared)


def forward_kernel(sizes, first_ref, shift_ref, *refs):
    cell_blocks, station_blocks, pairs, epochs, slots = sizes
    codes = refs[:slots]
    messages = refs[slots : 2 * slots]
    values_ref, turned_ref = refs[2 * slots : 2 * slots + 2]
    images = refs[2 * slots + 2 : 3 * slots + 2]
    list_ref, count_ref = refs[3 * slots + 2 : 3 * slots + 4]
    across_ref, along_ref, image_ref, high0, low0, high1, low1 = refs[3 * slots + 4 :]
    dummy = slots * station_blocks
    across_ref[pl.ds(dummy, 1), :] = jnp.zeros((1, SBLOCK), F32)
    along_ref[pl.ds(dummy, 1), :] = jnp.zeros((1, SBLOCK), F32)
    image_ref[...] = jnp.zeros_like(image_ref)
    count = jnp.int32(0)
    for slot in range(slots):
        for q in range(station_blocks):
            at = pl.ds(q * SBLOCK, SBLOCK)
            row = pl.ds(slot * station_blocks + q, 1)
            across_ref[row, :] = messages[slot][pl.ds(0, 1), at] + shift_ref[slot]
            along_ref[row, :] = messages[slot][pl.ds(1, 1), at]
        count = list_pairs(slot, first_ref, codes[slot], list_ref, count, cell_blocks, station_blocks, pairs)
    for i in range(4):
        list_ref[count + i] = dummy * cell_blocks
    count_ref[0] = count
    column = lax.broadcasted_iota(jnp.int32, (COL_SIDE, SBLOCK), 0).astype(F32)
    column = (column + 0.5) / COL_SIDE
    rows = CBLOCK // COL_SIDE

    def build(i, high_ref, low_ref):
        code = list_ref[i]
        q, w = code // cell_blocks, code % cell_blocks
        across = across_ref[pl.ds(q, 1), :] - column
        across = across * across
        along = along_ref[pl.ds(q, 1), :] - (w % 2).astype(F32) * (rows / COL_SIDE)
        turned = pltpu.roll(turned_ref[...], (LANES - w * (CBLOCK // LANES)) % LANES, 1)
        for y in range(rows):
            part = (y * COL_SIDE) // LANES
            at = (y * COL_SIDE) % LANES
            depth = jnp.broadcast_to(turned[at : at + COL_SIDE, part : part + 1], (COL_SIDE, SBLOCK))
            gap = along - (y + 0.5) / COL_SIDE
            high, low = split(inverse_cube((across + gap * gap) + depth))
            high_ref[pl.ds(y * COL_SIDE, COL_SIDE), :] = high
            low_ref[pl.ds(y * COL_SIDE, COL_SIDE), :] = low

    def multiply(i, high_ref, low_ref):
        code = list_ref[i]
        q, w = code // cell_blocks, code % cell_blocks
        values = values_ref[w]
        first = dot(values, high_ref[...])
        second = dot(values[:epochs], low_ref[...])
        image_ref[q] += first[:epochs] + first[epochs:] + second

    pipelined(count, build, multiply, ((high0, low0), (high1, low1)))
    for slot in range(slots):
        images[slot][...] = image_ref[pl.ds(slot * station_blocks, station_blocks)]


def forward(sizes, first, shift, messages, values, turned):
    cell_blocks, station_blocks, pairs, epochs, slots = sizes
    kernel_matrix = pltpu.VMEM((CBLOCK, SBLOCK), BF16)
    head = pl.BlockSpec((8, LANES), lambda i: (0, 0), memory_space=pltpu.SMEM)
    rows = (slots * station_blocks + 8) // 8 * 8
    return pl.pallas_call(
        functools.partial(forward_kernel, sizes),
        out_shape=(jax.ShapeDtypeStruct((station_blocks, epochs, SBLOCK), F32),) * slots
        + (
            jax.ShapeDtypeStruct((slots * station_blocks * pairs + 8,), jnp.int32),
            jax.ShapeDtypeStruct((1,), jnp.int32),
        ),
        grid=(1,),
        in_specs=[SMEM, SMEM] + [head] * slots + [VMEM] * (slots + 2),
        out_specs=(VMEM,) * slots + (SMEM, SMEM),
        scratch_shapes=[
            pltpu.VMEM((rows, SBLOCK), F32),
            pltpu.VMEM((rows, SBLOCK), F32),
            pltpu.VMEM((slots * station_blocks + 1, epochs, SBLOCK), F32),
        ]
        + [kernel_matrix] * 4,
        compiler_params=params(),
        cost_estimate=pl.CostEstimate(flops=5 * 10**9, bytes_accessed=2 * 10**6, transcendentals=8 * 10**6),
        name="forward",
    )(first, shift, *messages, *messages, values, turned)


def adjoint_kernel(sizes, list_ref, count_ref, shift_ref, *refs):
    cell_blocks, station_blocks, pairs, epochs, slots = sizes
    messages = refs[:slots]
    images = refs[slots : 2 * slots]
    cells_ref, model_ref, direction_ref, sums_ref = refs[2 * slots : 2 * slots + 4]
    constant_ref, slope_ref, stats_ref = refs[2 * slots + 4 : 2 * slots + 7]
    stations_ref, terms_ref, total_ref, high0, low0, high1, low1 = refs[2 * slots + 7 :]
    dummy = slots * station_blocks
    terms_ref[dummy] = jnp.zeros(terms_ref.shape[1:], BF16)
    stations_ref[slots] = jnp.zeros(stations_ref.shape[1:], F32)
    total_ref[...] = jnp.zeros_like(total_ref)
    per_block = SBLOCK // LANES
    lane_rows = station_blocks * per_block
    for slot in range(slots):
        parts = [messages[slot][pl.ds(0, 1), pl.ds(i * LANES, LANES)] + shift_ref[slot] for i in range(lane_rows)]
        parts += [messages[slot][pl.ds(1, 1), pl.ds(i * LANES, LANES)] for i in range(lane_rows)]
        parts.append(jnp.zeros((LANES - 2 * lane_rows, LANES), F32))
        stations_ref[slot] = jnp.concatenate(parts, axis=0).T
        for q in range(station_blocks):
            stacked = jnp.concatenate(
                [messages[slot][pl.ds(8, epochs), pl.ds(q * SBLOCK, SBLOCK)], images[slot][q]], axis=0
            )
            high, low = split(stacked)
            terms_ref[slot * station_blocks + q, pl.ds(0, 2 * epochs), :] = high
            terms_ref[slot * station_blocks + q, pl.ds(2 * epochs, 2 * epochs), :] = low
    lane = lax.broadcasted_iota(jnp.int32, (16, LANES), 1)
    column = ((lane % COL_SIDE).astype(F32) + 0.5) / COL_SIDE
    line = ((lane // COL_SIDE).astype(F32) + 0.5) / COL_SIDE
    rows = CBLOCK // COL_SIDE
    chunks = CBLOCK // LANES

    def build(i, high_ref, low_ref):
        code = list_ref[i]
        q, w = code // cell_blocks, code % cell_blocks
        slot, within = q // station_blocks, q % station_blocks
        at_cells = pl.ds(pl.multiple_of(w * CBLOCK, CBLOCK), CBLOCK)
        depth = cells_ref[pl.ds(0, 1), at_cells]
        half = (w % 2).astype(F32) * (rows / COL_SIDE)
        stations = pltpu.roll(stations_ref[slot], (LANES - within * per_block) % LANES, 1)
        for part in range(per_block):
            for at in range(0, LANES, 16):
                across = jnp.broadcast_to(stations[at : at + 16, part : part + 1], (16, LANES)) - column
                across = across * across
                part_along = lane_rows + part
                along = jnp.broadcast_to(stations[at : at + 16, part_along : part_along + 1], (16, LANES))
                along = along - (line + half)
                for chunk in range(chunks):
                    gap = along - chunk * (LANES // COL_SIDE) / COL_SIDE
                    squared = (across + gap * gap) + depth[:, chunk * LANES : (chunk + 1) * LANES]
                    high, low = split(inverse_cube(squared))
                    place = (pl.ds(part * LANES + at, 16), pl.ds(chunk * LANES, LANES))
                    high_ref[place] = high
                    low_ref[place] = low

    def multiply(i, high_ref, low_ref):
        code = list_ref[i]
        q, w = code // cell_blocks, code % cell_blocks
        terms = terms_ref[q]
        first = dot(terms, high_ref[...])
        second = dot(terms[: 2 * epochs], low_ref[...])
        total_ref[w] += first[: 2 * epochs] + first[2 * epochs :] + second

    pipelined(count_ref[0], build, multiply, ((high0, low0), (high1, low1)))

    zero = jnp.zeros((epochs, CBLOCK), F32)

    def combine(w, sums):
        at = pl.ds(pl.multiple_of(w * CBLOCK, CBLOCK), CBLOCK)
        total = total_ref[w] * cells_ref[pl.ds(1, 1), at]
        constant = total[:epochs] - DAMPING * model_ref[:, at]
        slope = total[epochs:] + DAMPING * direction_ref[:, at]
        constant_ref[:, at] = constant
        slope_ref[:, at] = slope
        return sums[0] + constant * slope, sums[1] + slope * slope

    cross, square = lax.fori_loop(0, cell_blocks, combine, (zero, zero), unroll=2)
    square = jnp.sum(square).reshape(1, 1)
    cross = jnp.sum(cross).reshape(1, 1)
    local_step = jnp.where(square > 0, cross / jnp.where(square > 0, square, 1.0), 0.0)

    def remainder(w, sums):
        at = pl.ds(pl.multiple_of(w * CBLOCK, CBLOCK), CBLOCK)
        slope = slope_ref[:, at]
        left = constant_ref[:, at] - local_step * slope
        return sums[0] + left * left, sums[1] + left * slope

    left_square, left_cross = lax.fori_loop(0, cell_blocks, remainder, (zero, zero), unroll=2)
    image = images[0][...]
    stats = [
        sums_ref[pl.ds(0, 1), pl.ds(0, 1)],
        sums_ref[pl.ds(1, 1), pl.ds(0, 1)],
        jnp.sum(image * image).reshape(1, 1),
        local_step,
        jnp.sum(left_square).reshape(1, 1),
        jnp.sum(left_cross).reshape(1, 1),
        jnp.sqrt(square),
        jnp.zeros((1, 1), F32),
    ]
    stats = jnp.concatenate([jnp.broadcast_to(value, (1, LANES)) for value in stats], axis=0)
    for i in range(stats_ref.shape[0]):
        stats_ref[i] = stats


def adjoint(sizes, ranks, pair_list, count, shift, messages, images, cell_rows, model_field, direction, sums):
    cell_blocks, station_blocks, pairs, epochs, slots = sizes
    kernel_matrix = pltpu.VMEM((SBLOCK, CBLOCK), BF16)
    return pl.pallas_call(
        functools.partial(adjoint_kernel, sizes),
        out_shape=(
            jax.ShapeDtypeStruct(model_field.shape, F32),
            jax.ShapeDtypeStruct(model_field.shape, F32),
            jax.ShapeDtypeStruct((ranks, 8, LANES), F32),
        ),
        in_specs=[SMEM] * 3 + [VMEM] * (2 * slots + 4),
        out_specs=(VMEM,) * 3,
        scratch_shapes=[
            pltpu.VMEM((slots + 1, LANES, LANES), F32),
            pltpu.VMEM((slots * station_blocks + 1, 4 * epochs, SBLOCK), BF16),
            pltpu.VMEM((cell_blocks, 2 * epochs, CBLOCK), F32),
        ]
        + [kernel_matrix] * 4,
        compiler_params=params(),
        cost_estimate=pl.CostEstimate(flops=5 * 10**9, bytes_accessed=6 * 10**6, transcendentals=8 * 10**6),
        name="adjoint",
    )(pair_list, count, shift, *messages, *images, cell_rows, model_field, direction, sums)


def finish_kernel(
    stats_ref, constant_ref, slope_ref, model_ref, direction_ref, residual_ref, image_ref, model_out, residual_out, direction_out
):
    totals = jnp.sum(stats_ref[...], axis=0)[:, :1]
    gamma_old = totals[0:1]
    step = gamma_old / (totals[2:3] + DAMPING * totals[1:2] + GUARD)
    stats = stats_ref[...]
    ahead = step[None] - stats[:, 3:4, :]
    reach = ahead * stats[:, 6:7, :]
    gamma_new = jnp.sum(stats[:, 4:5, :] - 2.0 * ahead * stats[:, 5:6, :] + reach * reach, axis=0)[:, :1]
    ratio = gamma_new / (gamma_old + GUARD)
    blocks = model_ref.shape[1] // CBLOCK

    def block(w, unused):
        at = pl.ds(pl.multiple_of(w * CBLOCK, CBLOCK), CBLOCK)
        direction = direction_ref[:, at]
        model_out[:, at] = model_ref[:, at] + step * direction
        direction_out[:, at] = (constant_ref[:, at] - step * slope_ref[:, at]) + ratio * direction
        return 0

    lax.fori_loop(0, blocks, block, 0, unroll=2)
    for q in range(image_ref.shape[0]):
        at = pl.ds(q * SBLOCK, SBLOCK)
        residual_out[:, at] = residual_ref[:, at] - step * image_ref[q]


def finish(stats, constant, slope, model_field, direction, residual, image):
    return pl.pallas_call(
        finish_kernel,
        out_shape=(
            jax.ShapeDtypeStruct(model_field.shape, F32),
            jax.ShapeDtypeStruct(residual.shape, F32),
            jax.ShapeDtypeStruct(direction.shape, F32),
        ),
        in_specs=[VMEM] * 7,
        out_specs=(VMEM,) * 3,
        compiler_params=params(),
        name="finish",
    )(stats, constant, slope, model_field, direction, residual, image)


def shards(model_field, direction, old_grad, residual, block_pairs, depth_band, station_offsets):
    ranks = lax.axis_size("tile")
    tile_id = lax.axis_index("tile")
    epochs, cells = model_field.shape
    stations = residual.shape[1]
    station_blocks, pairs = block_pairs.shape
    cell_blocks = cells // CBLOCK
    sizes = (cell_blocks, station_blocks, pairs, epochs, SLOTS)
    side = 2 * (tile_id % 2) - 1

    def to_partner(array):
        return lax.ppermute(array, "tile", [(i, i ^ 1) for i in range(ranks)])

    def across(array):
        ends = [(i, i + 1) for i in range(1, ranks - 1, 2)]
        return lax.ppermute(array, "tile", ends + [(j, i) for i, j in ends])

    codes = jnp.pad(block_pairs.reshape(1, -1).astype(F32) + 1.0, ((0, 0), (0, stations - station_blocks * pairs)))
    own = jnp.concatenate([station_offsets, codes, jnp.zeros((5, stations), F32), residual], axis=0)
    partner = to_partner(own)
    arrived = across(jnp.stack([own, partner]))
    first_far, second_far = arrived[0], arrived[1]
    third_far = to_partner(first_far)
    messages = [own, partner, first_far, second_far, third_far]
    offsets = jnp.stack([0 * side, -side, side, 2 * side, -2 * side]).astype(jnp.int32)
    first_code = cell_blocks * (REACH - offsets) + 1
    shift = offsets.astype(F32)

    values, cell_rows, turned, sums = prepare(2.0 / math.sqrt(cells), depth_band, direction, old_grad)
    outs = forward(sizes, first_code, shift, messages, values, turned)
    partials, (pair_list, count) = outs[:SLOTS], outs[SLOTS:]

    near = partials[2] + to_partner(partials[4])
    given = across(jnp.stack([near, partials[3]]))
    image = partials[0] + given[0] + to_partner(partials[1] + given[1])

    partner_image = to_partner(image)
    arrived = across(jnp.stack([image, partner_image]))
    images = [image, partner_image, arrived[0], arrived[1], to_partner(arrived[0])]

    constant, slope, stats = adjoint(
        sizes, ranks, pair_list, count, shift, messages, images, cell_rows, model_field, direction, sums
    )
    stats = lax.all_to_all(stats, "tile", 0, 0)
    return finish(stats, constant, slope, model_field, direction, residual, image)


def solution(mesh):
    wide = P(None, ("groups", "tile"))
    return jax.shard_map(
        shards,
        mesh=mesh,
        in_specs=(wide, wide, wide, wide, P(("groups", "tile"), None), P(("groups", "tile")), wide),
        out_specs=(wide, wide, wide),
        check_vma=False,
    )
```

time: 433 us -> 109 us (0.25)
  local copies, waits for them, and re-layouts: 128 us -> 1.55 us
  waiting for transfers between devices: 101 us -> 6.09 us
  matrix products: 63.8 us -> 0 us
  blocking collectives: 72.8 us -> 24.1 us
  other arithmetic: 35.3 us -> 1.92 us
  Pallas kernels: 0 us -> 32.9 us
  starting transfers between devices: 24.1 us -> 39.9 us
    ppermute x12 -> x9, waiting for transfers between devices: 101 us -> 6.09 us  [the longest x6 6.08 us: to_partner(): return lax.ppermute(array, 'tile', [(i, i ^ 1) for i in range(ranks)])]
    psum x2 -> x0, blocking collectives: 72.8 us -> none  [the longest x1 39.2 us: shards(): lax.psum((jnp.sum(old_grad * old_grad), jnp.sum(direction * direction), j...]
    dot_general x16 -> x0, matrix products: 63.8 us -> none  [the longest x8 34.8 us: forward_block(): jnp.einsum('epc,psc->es', gathered, matrix, precision=HIGHEST, preferred_...]
    gather x56 -> x0, local copies, waits for them, and re-layouts: 51.4 us -> none  [the longest x8 24.4 us: forward_block(): gathered = jnp.take(near_values, code_list, axis=1)]
    pallas_call x0 -> x4, Pallas kernels: none -> 32.9 us  [the longest x1 17 us: adjoint(): pl.pallas_call(functools.partial(adjoint_kernel, sizes), out_shape=(jax.S...]
    all_to_all x0 -> x1, blocking collectives: none -> 24.1 us  [shards(): stats = lax.all_to_all(stats, 'tile', 0, 0)]
    slice x1 -> x0, local copies, waits for them, and re-layouts: 19.8 us -> none  [slab_at(): return slab_stack[:, offset + REACH, :]]
    unnamed x19 -> x12, local copies, waits for them, and re-layouts: 20.4 us -> 1.26 us
  transfers between devices with their start and end apart: 12 -> 9, of which waited for: 4 -> 6; matrix products, arithmetic and copies ran while one was open for 3% -> 0% of each run, Pallas kernels for 0% -> 1%
where the time goes in v1:
time: 109 us; the launch traced here: 107 us
  starting transfers between devices  39.9 us (37%)
  Pallas kernels  32.9 us (30%)
  blocking collectives  24.1 us (22%)
  waiting for transfers between devices  6.09 us (6%)
  other arithmetic  1.92 us (2%)
  local copies, waits for them, and re-layouts  1.55 us (1%)
    ppermute x6, starting transfers between devices, to_partner(): return lax.ppermute(array, 'tile', [(i, i ^ 1) for i in range(ranks)])  37.8 us
    all_to_all x1, blocking collectives, shards(): stats = lax.all_to_all(stats, 'tile', 0, 0)  24.1 us
    pallas_call x1, Pallas kernels, adjoint(): pl.pallas_call(functools.partial(adjoint_kernel, sizes), out_shape=(jax.S...  17 us
    pallas_call x1, Pallas kernels, forward(): pl.pallas_call(functools.partial(forward_kernel, sizes), out_shape=(jax.S...  12.8 us
    ppermute x6, waiting for transfers between devices, to_partner(): return lax.ppermute(array, 'tile', [(i, i ^ 1) for i in range(ranks)])  6.08 us
    pallas_call x1, Pallas kernels, finish(): pl.pallas_call(finish_kernel, out_shape=(jax.ShapeDtypeStruct(model_field...  2.3 us
  transfers between devices with their start and end apart: 9, of which 6 were waited for; matrix products, arithmetic and copies ran while one was open for 0% of the time, Pallas kernels for 1%

profile of v1, /device:TPU:0, one launch (start us, length us, event | category | flops | bytes accessed | tf_op | source)
XLA Modules:
  0.0 107.3 jit_solution(15347691857094659133)
XLA Ops:
  0.7 0.8 convert_add_fusion
  1.4 0.1 add.43
  1.5 0.1 pad.13.clone
  1.6 1.0 fusion.6
  2.6 0.5 collective-permute-start
  3.1 1.1 collective-permute-done.refs_1_.refs_6_
  4.2 0.7 collective-permute-start.1
  4.9 0.1 stack.46
  5.0 0.0 copy-done.4
  5.0 1.2 %copy-done.2 = f32[16,16384]{1,0:T(8,128)S(1)} copy-done((f32[16,16384]{1,0:T(8,128)S(1)}, f32[16,16384]{1,0:T(8,128)}, u32[]{:S(2)}) %copy-start.2) | copy-done | bytes 1048600
  6.3 0.7 prepare.1
  7.0 0.0 collective-permute-done.1
  7.1 11.1 %collective-permute-start.2 = (f32[24,2048]{1,0:T(8,128)S(1)}, f32[24,2048]{1,0:T(8,128)S(1)}, u32[]{:S(2)}, u32[]{:S(2)}) collective-permute-start(f32[24,2048]{1,0:T(8,128)S(1)} %get-tuple-element.32.refs_2_.refs_7_), channel_id=1, source_target_pairs={{0,1},{1,0},{2,3},{3,2},{4,5},{5,4},{6,7},{7,6},{8,9},{9,8},{10,11... | collective-permute-start | bytes 589832 | tf_op jit(solution)/shard_map/ppermute | solution.py:378
  18.2 1.1 collective-permute-done.2.refs_4_.refs_9_
  19.2 12.8 %forward.1 = (f32[8,16,256]{2,1,0:T(8,128)S(1)}, f32[8,16,256]{2,1,0:T(8,128)S(1)}, f32[8,16,256]{2,1,0:T(8,128)S(1)}, f32[8,16,256]{2,1,0:T(8,128)S(1)}, f32[8,...) custom-call(s32[5]{0:T(128)S(1)} %get-tuple-element.38.first_ref, f32[5]{0:T(128)S(1)} %get-tuple-element.37.shift_ref, ...), custom_call_target="tpu_custom_call" | custom-call | flops 5000000000 | bytes 2000000 | tf_op jit(solution)/shard_map/forward/pallas_call | solution.py:177
  32.1 2.3 %collective-permute-start.3 = (f32[8,16,256]{2,1,0:T(8,128)S(1)}, f32[8,16,256]{2,1,0:T(8,128)S(1)}, u32[]{:S(2)}, u32[]{:S(2)}) collective-permute-start(f32[8,16,256]{2,1,0:T(8,128)S(1)} %get-tuple-element.23), channel_id=1, source_target_pairs={{0,1},{1,0},{2,3},{3,2},{4,5},{5,4},{6,7},{7,6},{8,9},{9,8},{10,11... | collective-permute-start | bytes 393224 | tf_op jit(solution)/shard_map/ppermute | solution.py:378
  34.3 1.0 collective-permute-done.3
  35.4 0.0 copy-start.1
  35.4 0.8 collective-permute-start.4
  36.2 0.0 collective-permute-done.4
  36.2 13.2 %collective-permute-start.5 = (f32[8,16,256]{2,1,0:T(8,128)S(1)}, f32[8,16,256]{2,1,0:T(8,128)S(1)}, u32[]{:S(2)}, u32[]{:S(2)}) collective-permute-start(f32[8,16,256]{2,1,0:T(8,128)S(1)} %fusion.3), channel_id=1, source_target_pairs={{0,1},{1,0},{2,3},{3,2},{4,5},{5,4},{6,7},{7,6},{8,9},{9,8},{10,11... | collective-permute-start | bytes 393224 | tf_op jit(solution)/shard_map/ppermute | solution.py:378
  49.5 1.0 collective-permute-done.5
  50.5 0.4 collective-permute-start.6
  50.9 1.0 collective-permute-done.6.refs_6_
  51.9 0.7 collective-permute-start.7
  52.6 0.0 collective-permute-done.7
  52.6 10.2 %collective-permute-start.8 = (f32[8,16,256]{2,1,0:T(8,128)S(1)}, f32[8,16,256]{2,1,0:T(8,128)S(1)}, u32[]{:S(2)}, u32[]{:S(2)}) collective-permute-start(f32[8,16,256]{2,1,0:T(8,128)S(1)} %get-tuple-element.34.refs_7_), channel_id=1, source_target_pairs={{0,1},{1,0},{2,3},{3,2},{4,5},{5,4},{6,7},{7,6},{8,9},{9,8},{10,11... | collective-permute-start | bytes 393224 | tf_op jit(solution)/shard_map/ppermute | solution.py:378
  62.9 1.0 collective-permute-done.8.refs_9_
  63.9 17.0 %adjoint.1 = (f32[16,16384]{1,0:T(8,128)S(1)}, f32[16,16384]{1,0:T(8,128)S(1)}, f32[16,8,128]{2,1,0:T(8,128)S(1)}) custom-call(s32[328]{0:T(512)S(1)} %get-tuple-element.19.list_ref, s32[1]{0:T(128)} %get-tuple-element.20.count_ref, f32[5]{0:T(128)S(1)} %get-tuple-element.37.shift_ref, f32[24,2048]{1,0:T(8,128)S(1)} %get-tuple-element.36.refs_0_.refs_5_, ...), custom_call_target="tpu_custom_call" | custom-call | flops 5000000000 | bytes 6000000 | tf_op jit(solution)/shard_map/adjoint/pallas_call | solution.py:305
  80.9 0.0 copy-start.3
  80.9 24.1 %all_to_all.5.stats_ref = f32[16,8,128]{2,1,0:T(8,128)S(1)} all-to-all(f32[16,8,128]{2,1,0:T(8,128)S(1)} %get-tuple-element.28), channel_id=1, replica_groups=mesh['groups'=2,'tile'=16] {'tile'}, dimensions={0} | all-to-all | bytes 131072 | tf_op jit(solution)/shard_map/all_to_all | solution.py:410
  105.0 2.3 %finish.1 = (f32[16,16384]{1,0:T(8,128)}, f32[16,2048]{1,0:T(8,128)}, f32[16,16384]{1,0:T(8,128)}) custom-call(f32[16,8,128]{2,1,0:T(8,128)S(1)} %all_to_all.5.stats_ref, f32[16,16384]{1,0:T(8,128)S(1)} %get-tuple-element.29.constant_ref, f32[16,16384]{1,0:T(8,128)S(1)} %get-tuple-element.30.slope_ref, f32[16,16384]{1,0:T(8,128)S(1)} %copy-done.1, ...), custom_call_target="tpu_custom_call" | custom-call | tf_op jit(solution)/shard_map/finish/pallas_call | solution.py:353
  (18 shorter events, 0.2 us)
Async XLA Ops:
  0.6 1.0 copy-start.5
  0.6 4.4 %copy-start = (f32[16,16384]{1,0:T(8,128)S(1)}, f32[16,16384]{1,0:T(8,128)}, u32[]{:S(2)}) copy-start(f32[16,16384]{1,0:T(8,128)} %direction_ref.3) | copy-start | bytes 3145732
  2.6 1.6 %collective-permute-start = (f32[24,2048]{1,0:T(8,128)S(1)}, f32[24,2048]{1,0:T(8,128)S(1)}, u32[]{:S(2)}, u32[]{:S(2)}) collective-permute-start(f32[24,2048]{1,0:T(8,128)S(1)} %get-tuple-element.36.refs_0_.refs_5_), channel_id=1, source_target_pairs={{0,1},{1,0},{2,3},{3,2},{4,5},{5,4},{6,7},{7,6},{8,9},{9,8},{10,11... | collective-permute-start | bytes 589832 | tf_op jit(solution)/shard_map/ppermute | solution.py:378
  4.2 0.8 copy-start.4
  4.2 2.8 %collective-permute-start.1 = (f32[2,24,2048]{2,1,0:T(8,128)S(1)}, f32[2,24,2048]{2,1,0:T(8,128)S(1)}, u32[]{:S(2)}, u32[]{:S(2)}) collective-permute-start(f32[2,24,2048]{2,1,0:T(8,128)S(1)} %pad_maximum_fusion), channel_id=1, source_target_pairs={{1,2},{3,4},{5,6},{7,8},{9,10},{11,12},{13,14},{2,1},{4,3},{6,5},{... | collective-permute-start | bytes 1179656 | tf_op jit(solution)/shard_map/ppermute | solution.py:382
  5.0 1.2 %copy-start.2 = (f32[16,16384]{1,0:T(8,128)S(1)}, f32[16,16384]{1,0:T(8,128)}, u32[]{:S(2)}) copy-start(f32[16,16384]{1,0:T(8,128)} %old_ref.1) | copy-start | bytes 3145732
  7.1 12.2 %collective-permute-start.2 = (f32[24,2048]{1,0:T(8,128)S(1)}, f32[24,2048]{1,0:T(8,128)S(1)}, u32[]{:S(2)}, u32[]{:S(2)}) collective-permute-start(f32[24,2048]{1,0:T(8,128)S(1)} %get-tuple-element.32.refs_2_.refs_7_), channel_id=1, source_target_pairs={{0,1},{1,0},{2,3},{3,2},{4,5},{5,4},{6,7},{7,6},{8,9},{9,8},{10,11... | collective-permute-start | bytes 589832 | tf_op jit(solution)/shard_map/ppermute | solution.py:378
  32.1 3.3 %collective-permute-start.3 = (f32[8,16,256]{2,1,0:T(8,128)S(1)}, f32[8,16,256]{2,1,0:T(8,128)S(1)}, u32[]{:S(2)}, u32[]{:S(2)}) collective-permute-start(f32[8,16,256]{2,1,0:T(8,128)S(1)} %get-tuple-element.23), channel_id=1, source_target_pairs={{0,1},{1,0},{2,3},{3,2},{4,5},{5,4},{6,7},{7,6},{8,9},{9,8},{10,11... | collective-permute-start | bytes 393224 | tf_op jit(solution)/shard_map/ppermute | solution.py:378
  35.4 28.5 %copy-start.1 = (f32[16,16384]{1,0:T(8,128)S(1)}, f32[16,16384]{1,0:T(8,128)}, u32[]{:S(2)}) copy-start(f32[16,16384]{1,0:T(8,128)} %model_ref.1) | copy-start | bytes 3145732
  35.4 0.8 collective-permute-start.4
  36.2 14.2 %collective-permute-start.5 = (f32[8,16,256]{2,1,0:T(8,128)S(1)}, f32[8,16,256]{2,1,0:T(8,128)S(1)}, u32[]{:S(2)}, u32[]{:S(2)}) collective-permute-start(f32[8,16,256]{2,1,0:T(8,128)S(1)} %fusion.3), channel_id=1, source_target_pairs={{0,1},{1,0},{2,3},{3,2},{4,5},{5,4},{6,7},{7,6},{8,9},{9,8},{10,11... | collective-permute-start | bytes 393224 | tf_op jit(solution)/shard_map/ppermute | solution.py:378
  50.5 1.4 %collective-permute-start.6 = (f32[8,16,256]{2,1,0:T(8,128)S(1)}, f32[8,16,256]{2,1,0:T(8,128)S(1)}, u32[]{:S(2)}, u32[]{:S(2)}) collective-permute-start(f32[8,16,256]{2,1,0:T(8,128)S(1)} %fusion.5.refs_5_.image_ref), channel_id=1, source_target_pairs={{0,1},{1,0},{2,3},{3,2},{4,5},{5,4},{6,7},{7,6},{8,9},{9,8},{10,11... | collective-permute-start | bytes 393224 | tf_op jit(solution)/shard_map/ppermute | solution.py:378
  51.9 0.7 collective-permute-start.7
  52.6 11.2 %collective-permute-start.8 = (f32[8,16,256]{2,1,0:T(8,128)S(1)}, f32[8,16,256]{2,1,0:T(8,128)S(1)}, u32[]{:S(2)}, u32[]{:S(2)}) collective-permute-start(f32[8,16,256]{2,1,0:T(8,128)S(1)} %get-tuple-element.34.refs_7_), channel_id=1, source_target_pairs={{0,1},{1,0},{2,3},{3,2},{4,5},{5,4},{6,7},{7,6},{8,9},{9,8},{10,11... | collective-permute-start | bytes 393224 | tf_op jit(solution)/shard_map/ppermute | solution.py:378
  80.9 24.1 %copy-start.3 = (f32[16,2048]{1,0:T(8,128)S(1)}, f32[16,2048]{1,0:T(8,128)}, u32[]{:S(2)}) copy-start(f32[16,2048]{1,0:T(8,128)} %residual_ref.1) | copy-start | bytes 393220
